TPU v7x, 32 devices: a whole 2x2x4 slice. The times are simulated.
32 devices in a mesh: cube: 32 (over z, y, x, core).
Axes of the slice: x: 2, y: 2, z: 4, core: 2. Of those that a mesh axis runs over, the one named last changes fastest.
Arguments:
- gfront: float32 [8192, 2048], P('cube'), as said below
- cfront: float32 [8192, 4096], P('cube'), as said below
- rfront: float32 [8192, 8192], P('cube'), as said below
- gmap: int32 [4, 2048], replicated, may hold values from 0 to 4095, as said below
- cmap: int32 [2, 4096], replicated, may hold values from 0 to 8191, as said below
Outputs:
- gfactor: float32 [8192, 256], P('cube')
- cfactor: float32 [8192, 256], P('cube')
- rfactor: float32 [8192, 512], P('cube')
- rschur: float32 [8192, 8192], P('cube')
Inputs may be any that keep to these rules, and one draw needn't show every extreme that they name: Entry i of row q goes to a row of the parent front in block b or block b + 8, where b = i // 256 and blocks have 256 rows; within one row of gmap the entries are distinct and increase along each block. Entry i of row c goes to a row of the root front in block b or block b + 16, where b = i // 256 and blocks have 256 rows; within one row of cmap the entries are distinct and increase along each block. `gfront`: every front is symmetric and positive definite. `cfront`: every front is symmetric and positive definite. `rfront`: the front is symmetric and positive definite.
All inputs are finite; a program needn't handle non-finite values.
Results may differ from a plain program's by a relative error of at most 0.0003.
Values sent between devices are 32-bit elements; how exact they have to be, the bound alone decides.
No kernel may reach another device: no remote copies, remote signals or barrier semaphores. Data moves between devices by JAX's collectives and lax.ppermute only.
A program may use at most 128 MiB of HBM per device.

v0:
```python
import jax
import jax.numpy as jnp
from jax import lax
from jax.sharding import PartitionSpec as P

TILE = 256
PG = 1
PC = 1
PR = 2


def from_partner(value, axis, bit):
    mask = 2**bit
    pairs = [(source, source ^ mask) for source in range(lax.axis_size(axis))]
    return lax.ppermute(value, axis, pairs)


def share_panel(own_cols, group):
    device_idx = lax.axis_index("cube")
    everything = lax.all_gather(own_cols, "cube", axis=0, tiled=True)
    row_count = own_cols.shape[0]
    start_row = device_idx // group * group * row_count
    return lax.dynamic_slice_in_dim(everything, start_row, group * row_count, 0)


def kept_index(index_vals, order, separator):
    return (index_vals < order - separator - TILE) | (index_vals >= order - TILE)


def eliminate(rows_mat, panels, group):
    row_count = rows_mat.shape[0]
    order = rows_mat.shape[1]
    start = order - (panels + 1) * TILE
    device_idx = lax.axis_index("cube")
    row_ids = device_idx % group * row_count + jnp.arange(row_count, dtype=jnp.int32)
    col_ids = jnp.arange(order, dtype=jnp.int32)
    pieces = []
    for panel_no in range(panels):
        col_low = start + panel_no * TILE
        col_high = col_low + TILE
        own_cols = rows_mat[:, col_low:col_high]
        whole_panel = share_panel(own_cols, group)
        lower_tri = jnp.linalg.cholesky(whole_panel[col_low:col_high])
        weights = jax.scipy.linalg.cho_solve((lower_tri, True), own_cols.T).T
        factor = jax.scipy.linalg.solve_triangular(lower_tri, own_cols.T, lower=True).T
        pieces.append(jnp.where(((row_ids >= col_low) | (row_ids < start))[:, None], factor, 0.0))
        product = jnp.einsum("rb,nb->rn", weights, whole_panel, precision=lax.Precision.HIGHEST)
        row_rest = (row_ids >= col_high) | (row_ids < start)
        col_rest = (col_ids >= col_high) | (col_ids < start)
        trailing = row_rest[:, None] & col_rest[None, :]
        rows_mat = rows_mat - jnp.where(trailing, product, 0.0)
    return (rows_mat, jnp.concatenate(pieces, 1))


def extend_add(rows_mat, separator, maps_all, group):
    row_count = rows_mat.shape[0]
    order = rows_mat.shape[1]
    pair_bit = group.bit_length() - 1
    device_idx = lax.axis_index("cube")
    block_no = device_idx % group
    front_no = device_idx // group
    side = front_no % 2
    row_ids = block_no * row_count + jnp.arange(row_count, dtype=jnp.int32)
    col_ids = jnp.arange(order, dtype=jnp.int32)
    keep_mask = (
        kept_index(row_ids, order, separator)[:, None]
        & kept_index(col_ids, order, separator)[None, :]
    )
    masked = jnp.where(keep_mask, rows_mat, 0.0)
    own_map = lax.dynamic_index_in_dim(maps_all, front_no, 0, keepdims=False)
    widened = jnp.zeros((row_count, 2 * order), jnp.float32).at[:, own_map].add(masked)
    row_map = lax.dynamic_slice_in_dim(own_map, block_no * row_count, row_count, 0)
    slots = jnp.where(
        row_map < (block_no + 1) * row_count,
        row_map - block_no * row_count,
        row_map - (group + block_no) * row_count + row_count,
    )
    own_pair = jnp.zeros((2 * row_count, 2 * order), jnp.float32).at[slots].add(widened)
    kept_rows = lax.dynamic_slice_in_dim(own_pair, side * row_count, row_count, 0)
    outgoing = lax.dynamic_slice_in_dim(own_pair, (1 - side) * row_count, row_count, 0)
    received = from_partner(outgoing, "cube", pair_bit)
    return (kept_rows, received)


def local(gfront, cfront, rfront, gmap, cmap):
    devices = lax.axis_size("cube")
    quarter = devices // 4
    half_cube = devices // 2
    g_rows, gfactor = eliminate(gfront, PG, quarter)
    kept_rows, received = extend_add(g_rows, PG * TILE, gmap, quarter)
    c_rows = cfront + kept_rows + received
    c_done, cfactor = eliminate(c_rows, PC, half_cube)
    kept_rows, received = extend_add(c_done, PC * TILE, cmap, half_cube)
    r_rows = rfront + kept_rows + received
    r_done, rfactor = eliminate(r_rows, PR, devices)
    row_count = r_done.shape[0]
    order = r_done.shape[1]
    row_ids = lax.axis_index("cube") * row_count + jnp.arange(row_count, dtype=jnp.int32)
    col_ids = jnp.arange(order, dtype=jnp.int32)
    rest_mask = (
        kept_index(row_ids, order, PR * TILE)[:, None]
        & kept_index(col_ids, order, PR * TILE)[None, :]
    )
    rschur = jnp.where(rest_mask, r_done, 0.0)
    return (gfactor, cfactor, rfactor, rschur)


def solution(mesh):
    placed = (P("cube", None), P("cube", None), P("cube", None), P(), P())
    return jax.shard_map(
        local,
        mesh=mesh,
        in_specs=placed,
        out_specs=(P("cube", None), P("cube", None), P("cube", None), P("cube", None)),
        check_vma=False,
    )
```

profile of v0, /device:TPU:0, one launch (start us, length us, event | category | flops | bytes accessed | tf_op | source)
XLA Modules:
  0.0 1285.5 jit_solution(4973847167212889612)
XLA Ops:
  10.8 87.9 %all-gather.5.cloned.1.call-done = f32[8192,256]{0,1:T(8,128)} async-done(((f32[256,256]{0,1:T(8,128)}), f32[8192,256]{0,1:T(8,128)}) %all-gather.5.cloned.1.call-update) | async-done | bytes 8388624 | tf_op jit(solution)/shard_map/all_gather | solution.py:20
  100.8 11.7 cholesky.214
  122.9 11.7 cholesky.231
  141.2 19.7 %custom-call.32 = f32[2,128,128]{1,2,0:T(8,128)S(1)} custom-call(f32[2,128,128]{2,1,0:T(8,128)S(1)} %get-tuple-element.87), custom_call_target="InvertDiagBlocksLowerTriangular" | custom-call | tf_op jit(solution)/shard_map/jit(_solve_triangular)/triangular_solve/custom-call.1 | solution.py:45
  170.7 14.2 %scatter_custom_fusion = f32[256,4096]{0,1:T(8,128)} fusion(s32[2048]{0:T(1024)S(1)} %bitcast.221, f32[2048,256]{1,0:T(8,128)} %copy.26, f32[]{:T(128)} %constant.214.clone.1), kind=kCustom, calls=%fused_computation.34 | custom fusion | flops 524288 | bytes 4194816 | tf_op jit(solution)/shard_map/scatter-add | solution.py:71
  190.7 11.4 scatter_custom_fusion.1
  226.6 81.8 %collective-permute-done = f32[256,4096]{0,1:T(8,128)} collective-permute-done((f32[256,4096]{0,1:T(8,128)}, f32[256,4096]{0,1:T(8,128)}, u32[]{:S(2)}, u32[]{:S(2)}) %collective-permute-start) | collective-permute-done | bytes 4194336 | tf_op jit(solution)/shard_map/ppermute | solution.py:15
  317.1 82.3 %all-gather.7.cloned.1.call-done = f32[8192,256]{0,1:T(8,128)} async-done(((f32[256,256]{0,1:T(8,128)}), f32[8192,256]{0,1:T(8,128)}) %all-gather.7.cloned.1.call-update) | async-done | bytes 8388624 | tf_op jit(solution)/shard_map/all_gather | solution.py:20
  401.6 11.7 cholesky.248
  423.7 11.7 cholesky.265
  442.5 19.7 %custom-call.36 = f32[2,128,128]{1,2,0:T(8,128)S(1)} custom-call(f32[2,128,128]{2,1,0:T(8,128)S(1)} %get-tuple-element.90), custom_call_target="InvertDiagBlocksLowerTriangular" | custom-call | tf_op jit(solution)/shard_map/jit(_solve_triangular)/triangular_solve/custom-call.1 | solution.py:45
  475.2 26.7 %scatter_custom_fusion.2 = f32[256,8192]{0,1:T(8,128)} fusion(s32[4096]{0:T(1024)S(1)} %bitcast.220, f32[4096,256]{1,0:T(8,128)} %fusion.7, f32[]{:T(128)} %constant.214.clone.1), kind=kCustom, calls=%fused_computation.24 | custom fusion | flops 1048576 | bytes 8389120 | tf_op jit(solution)/shard_map/scatter-add | solution.py:71
  511.1 19.7 %scatter_custom_fusion.3 = f32[512,8192]{1,0:T(8,128)} fusion(s32[256]{0:T(256)S(1)} %bitcast.223, f32[256,8192]{1,0:T(8,128)} %copy.33, f32[]{:T(128)} %constant.214.clone.1), kind=kCustom, calls=%fused_computation.18 | custom fusion | flops 2097152 | bytes 16777728 | tf_op jit(solution)/shard_map/scatter-add | solution.py:78
  570.6 343.2 %collective-permute-done.1 = f32[256,8192]{0,1:T(8,128)} collective-permute-done((f32[256,8192]{0,1:T(8,128)}, f32[256,8192]{0,1:T(8,128)}, u32[]{:S(2)}, u32[]{:S(2)}) %collective-permute-start.1) | collective-permute-done | bytes 8388640 | tf_op jit(solution)/shard_map/ppermute | solution.py:15
  927.3 83.4 %all-gather.9.cloned.1.call-done = f32[8192,256]{0,1:T(8,128)} async-done(((f32[256,256]{0,1:T(8,128)}), f32[8192,256]{0,1:T(8,128)}) %all-gather.9.cloned.1.call-update) | async-done | bytes 8388624 | tf_op jit(solution)/shard_map/all_gather | solution.py:20
  1012.8 11.7 cholesky.282
  1034.9 11.7 cholesky.299
  1053.7 19.7 %custom-call.40 = f32[2,128,128]{1,2,0:T(8,128)S(1)} custom-call(f32[2,128,128]{2,1,0:T(8,128)S(1)} %get-tuple-element.93), custom_call_target="InvertDiagBlocksLowerTriangular" | custom-call | tf_op jit(solution)/shard_map/jit(_solve_triangular)/triangular_solve/custom-call.1 | solution.py:45
  1075.1 21.4 %fusion = f32[256,8192]{0,1:T(8,128)S(1)} fusion(f32[256,8192]{0,1:T(8,128)} %copy-done.1, f32[8192,256]{0,1:T(8,128)} %all-gather.9.cloned.1.call-done, pred[256]{0:T(512)(128)(4,1)S(1)} %compare_or_fusion.2, pred[8192]{0:T(1024)(128)(4,1)S(1)} %fusion.83, f32[128,256]{1,0:T(8,128)S(1)} %fusion.68, f32[128,256]{1,0:T(8,128)S(1)} %fusion.67), kind=kOutput, calls=%fused_computation.14 | convolution fusion | flops 6448807936 | bytes 25436416 | tf_op jit(solution)/shard_map/rb,nb->rn/dot_general | solution.py:47
  1102.5 81.0 %all-gather.11.cloned.1.call-done = f32[8192,256]{0,1:T(8,128)} async-done(((f32[256,256]{0,1:T(8,128)}), f32[8192,256]{0,1:T(8,128)}) %all-gather.11.cloned.1.call-update) | async-done | bytes 8388624 | tf_op jit(solution)/shard_map/all_gather | solution.py:20
  1185.7 11.7 cholesky.316
  1207.7 11.7 cholesky.333
  1225.9 19.9 %custom-call.44 = f32[2,128,128]{1,2,0:T(8,128)S(1)} custom-call(f32[2,128,128]{2,1,0:T(8,128)S(1)} %get-tuple-element.96), custom_call_target="InvertDiagBlocksLowerTriangular" | custom-call | tf_op jit(solution)/shard_map/jit(_solve_triangular)/triangular_solve/custom-call.1 | solution.py:45
  1248.6 21.2 %fusion.2 = f32[256,8192]{0,1:T(8,128)} fusion(f32[256,8192]{0,1:T(8,128)} %copy-done, f32[8192,256]{0,1:T(8,128)} %all-gather.11.cloned.1.call-done, pred[256]{0:T(512)(128)(4,1)S(1)} %get-tuple-element.183, pred[256]{0:T(512)(128)(4,1)S(1)} %get-tuple-element.184, pred[8192]{0:T(1024)(128)(4,1)S(1)} %fusion.82, f32[128,256]{1,0:T(8,128)S(1)} %fusion.70, ...), kind=kOutput, calls=%fused_computation.16 | convolution fusion | flops 6453002240 | bytes 25436672 | tf_op jit(solution)/shard_map/rb,nb->rn/dot_general | solution.py:47
  (171 shorter events, 234.1 us)
Async XLA Ops:
  7.2 91.6 %all-gather.5.cloned.1.call-start = ((), (), s32[]{:S(2)}) async-start(), calls=%async_computation | async-start | bytes 8650752 | tf_op jit(solution)/shard_map/all_gather | solution.py:20
  9.0 390.4 %all-gather.7.cloned.1.call-start = ((), (), s32[]{:S(2)}) async-start(), calls=%async_computation.1 | async-start | bytes 8650752 | tf_op jit(solution)/shard_map/all_gather | solution.py:20
  215.3 93.1 %collective-permute-start = (f32[256,4096]{0,1:T(8,128)}, f32[256,4096]{0,1:T(8,128)}, u32[]{:S(2)}, u32[]{:S(2)}) collective-permute-start(f32[256,4096]{0,1:T(8,128)} %copy.50), channel_id=1, source_target_pairs={{0,8},{1,9},{2,10},{3,11},{4,12},{5,13},{6,14},{7,15},{8,0},{9,1},... | collective-permute-start | bytes 12582920 | tf_op jit(solution)/shard_map/ppermute | solution.py:15
  226.6 90.4 %copy-start.3 = (s32[2,4096]{1,0:T(2,128)S(1)}, s32[2,4096]{1,0:T(2,128)}, u32[]{:S(2)}) copy-start(s32[2,4096]{1,0:T(2,128)} %param.14) | copy-start | bytes 98308
  313.9 2.0 copy-start.2
  316.7 694.0 %all-gather.9.cloned.1.call-start = ((), (), s32[]{:S(2)}) async-start(), calls=%async_computation.2 | async-start | bytes 8650752 | tf_op jit(solution)/shard_map/all_gather | solution.py:20
  551.1 362.7 %collective-permute-start.1 = (f32[256,8192]{0,1:T(8,128)}, f32[256,8192]{0,1:T(8,128)}, u32[]{:S(2)}, u32[]{:S(2)}) collective-permute-start(f32[256,8192]{0,1:T(8,128)} %copy.52), channel_id=1, source_target_pairs={{0,16},{1,17},{2,18},{3,19},{4,20},{5,21},{6,22},{7,23},{8,24},{9,... | collective-permute-start | bytes 25165832 | tf_op jit(solution)/shard_map/ppermute | solution.py:15
  922.8 3.4 copy-start.1
  927.0 256.6 %all-gather.11.cloned.1.call-start = ((), (), s32[]{:S(2)}) async-start(), calls=%async_computation.3 | async-start | bytes 8650752 | tf_op jit(solution)/shard_map/all_gather | solution.py:20
  1096.5 3.4 copy-start
Sparse Core Ops, SparseCore 0:
  11.5 87.2 all-gather.4
  316.8 82.6 all-gather.6
  927.1 83.5 all-gather.8
  1100.8 82.6 all-gather.10
where the time goes:
time: 1290 us
  waiting for transfers between devices  760 us (59%)
  other arithmetic  309 us (24%)
  local copies, waits for them, and re-layouts  124 us (10%)
  matrix products  68.8 us (5%)
  between operations  20 us (2%)
    ppermute x2, waiting for transfers between devices, from_partner(): return lax.ppermute(value, axis, pairs)  425 us
    all_gather x4, waiting for transfers between devices, share_panel(): everything = lax.all_gather(own_cols, 'cube', axis=0, tiled=True)  335 us
    another operation x27, other arithmetic, eliminate(): lower_tri = jnp.linalg.cholesky(whole_panel[col_low:col_high])  138 us
    another operation x9, other arithmetic, eliminate(): jax.scipy.linalg.solve_triangular(lower_tri, own_cols.T, lower=True)  79 us
    unnamed x19, local copies, waits for them, and re-layouts  65 us
    dot_general x4, matrix products, eliminate(): jnp.einsum('rb,nb->rn', weights, whole_panel, precision=lax.Precision.HIG...  58.3 us
    scatter-add x2, other arithmetic, extend_add(): jnp.zeros((row_count, 2 * order), jnp.float32).at[:, own_map].add(masked)  40.9 us
    scatter-add x2, other arithmetic, extend_add(): jnp.zeros((2 * row_count, 2 * order), jnp.float32).at[slots].add(widened)  31.1 us
  transfers between devices with their start and end apart: 6, of which 6 were waited for; matrix products, arithmetic and copies ran while one was open for 3% of the time, Pallas kernels for 0%

commit v1 on v0

v1 whole, which is shorter than its diff:
```python
import functools

import jax
import jax.numpy as jnp
from jax import lax
from jax.experimental import pallas as pl
from jax.experimental.pallas import tpu as pltpu
from jax.sharding import PartitionSpec as P

TILE = 256
STRIP = 32
SUB = 8
LANES = 128
HIGH = lax.Precision.HIGH
HIGHEST = lax.Precision.HIGHEST
NT = (((1,), (1,)), ((), ()))
MIB = 1024 * 1024


def widen(column, width):
    return jnp.concatenate([column] * (width // LANES), 1)


def factor_strip(strip, base):
    width = strip[0].shape[1]
    sub_ids = lax.broadcasted_iota(jnp.int32, (SUB, 1), 0)
    count = len(strip)
    for p in range(count):
        first = base + p * SUB
        cols = [
            [jnp.broadcast_to(strip[q][:, first + j : first + j + 1], (SUB, LANES)) for j in range(SUB)]
            for q in range(p, count)
        ]
        for j in range(SUB):
            pivot = cols[0][j][j : j + 1, :]
            inv = lax.rsqrt(pivot)
            inv = inv * (1.5 - 0.5 * pivot * inv * inv)
            unit = strip[p][j : j + 1, :] * widen(inv, width)
            scaled = [col[j] * inv for col in cols]
            below = jnp.where(sub_ids > j, scaled[0], 0.0)
            strip[p] = jnp.where(sub_ids == j, unit, strip[p] - widen(below, width) * unit)
            for q in range(p + 1, count):
                strip[q] = strip[q] - widen(scaled[q - p], width) * unit
            for m in range(j + 1, SUB):
                head = scaled[0][m : m + 1, :]
                for q in range(p, count):
                    cols[q - p][m] = cols[q - p][m] - scaled[q - p] * head
    return jnp.concatenate(strip, 0)


def inverse_kernel(count, blocks_ref, inverse_ref, work):
    row_ids = lax.broadcasted_iota(jnp.int32, (TILE, TILE), 0)
    col_ids = lax.broadcasted_iota(jnp.int32, (TILE, TILE), 1)
    for t in range(count):
        work[t, :, :TILE] = blocks_ref[t]
        work[t, :, TILE:] = (row_ids == col_ids).astype(jnp.float32)
    for low in range(0, TILE, STRIP):
        high = low + STRIP
        left = low // LANES * LANES
        right = TILE + (high + LANES - 1) // LANES * LANES
        done = []
        for t in range(count):
            strip = [work[t, low + SUB * q : low + SUB * (q + 1), left:right] for q in range(STRIP // SUB)]
            done.append(factor_strip(strip, low - left))
        for t in range(count):
            inverse_ref[t, low:high, : right - TILE] = done[t][:, TILE - left :]
            if right < 2 * TILE:
                inverse_ref[t, low:high, right - TILE :] = jnp.zeros((STRIP, 2 * TILE - right), jnp.float32)
            if high < TILE:
                rest = high // LANES * LANES
                update = lax.dot_general(
                    done[t][:, rest - left : TILE - left],
                    done[t],
                    (((0,), (0,)), ((), ())),
                    precision=HIGHEST,
                    preferred_element_type=jnp.float32,
                )
                work[t, high:, left:right] = work[t, high:, left:right] - update[high - rest :]


def inverse_factors(blocks):
    count = blocks.shape[0]
    return pl.pallas_call(
        functools.partial(inverse_kernel, count),
        out_shape=jax.ShapeDtypeStruct(blocks.shape, jnp.float32),
        in_specs=[pl.BlockSpec(memory_space=pltpu.VMEM)],
        out_specs=pl.BlockSpec(memory_space=pltpu.VMEM),
        scratch_shapes=[pltpu.VMEM((count, TILE, 2 * TILE), jnp.float32)],
        compiler_params=pltpu.CompilerParams(vmem_limit_bytes=16 * MIB),
        cost_estimate=pl.CostEstimate(flops=30_000_000_000, bytes_accessed=1_000_000, transcendentals=0),
    )(blocks)


def halves(value):
    top = value.astype(jnp.bfloat16)
    return top, (value - top.astype(jnp.float32)).astype(jnp.bfloat16)


def dot_nt(left, right):
    return lax.dot_general(left, right, NT, preferred_element_type=jnp.float32)


def dot_nn(left, right):
    return jnp.dot(left, right, preferred_element_type=jnp.float32)


def assemble_kernel(base_ref, keep_ref, recv_ref, place_ref, keep_map_ref, recv_map_ref, out_ref):
    first = pl.program_id(0) * TILE
    targets = first + lax.broadcasted_iota(jnp.int32, (TILE, TILE), 0)
    keep_hot = jnp.where(keep_map_ref[...] == targets, 1.0, 0.0).astype(jnp.bfloat16)
    recv_hot = jnp.where(recv_map_ref[...] == targets, 1.0, 0.0).astype(jnp.bfloat16)
    top, rest = halves(keep_ref[...])
    total = base_ref[...] + (dot_nt(top, keep_hot) + dot_nt(rest, keep_hot))
    top, rest = halves(recv_ref[...])
    moved = dot_nt(top, recv_hot) + dot_nt(rest, recv_hot)
    top, rest = halves(moved)
    place = place_ref[...]
    out_ref[...] = total + (dot_nn(place, top) + dot_nn(place, rest))


def assemble(base, keep, recv, place, keep_map, recv_map):
    rows, order = base.shape
    sent = recv.shape[0]
    child_blocks = order // 2 // TILE
    return pl.pallas_call(
        assemble_kernel,
        grid=(order // TILE,),
        out_shape=jax.ShapeDtypeStruct(base.shape, jnp.float32),
        in_specs=[
            pl.BlockSpec((rows, TILE), lambda n: (0, n)),
            pl.BlockSpec((rows, TILE), lambda n: (0, n % child_blocks)),
            pl.BlockSpec((sent, TILE), lambda n: (0, n % child_blocks)),
            pl.BlockSpec((rows, sent), lambda n: (0, 0)),
            pl.BlockSpec((1, TILE), lambda n: (0, n % child_blocks)),
            pl.BlockSpec((1, TILE), lambda n: (0, n % child_blocks)),
        ],
        out_specs=pl.BlockSpec((rows, TILE), lambda n: (0, n)),
        compiler_params=pltpu.CompilerParams(vmem_limit_bytes=24 * MIB),
        cost_estimate=pl.CostEstimate(
            flops=2 * rows * order * TILE * 6, bytes_accessed=rows * order * 12, transcendentals=0
        ),
    )(base, keep, recv, place, keep_map, recv_map)


def finish_kernel(low, high, base_ref, rows_ref, first_ref, second_ref, weights_ref, out_ref, top_ref, rest_ref):
    block = pl.program_id(0)

    @pl.when(block == 0)
    def _():
        top_ref[...], rest_ref[...] = halves(weights_ref[...])

    rows = rows_ref.shape[0]
    row_ids = base_ref[0] + lax.broadcasted_iota(jnp.int32, (rows, 1), 0)
    kept = (row_ids < low) | (row_ids >= high)
    inside = (block >= low // TILE) & (block < high // TILE)

    @pl.when(inside)
    def _():
        out_ref[...] = jnp.zeros_like(out_ref)

    @pl.when(jnp.logical_not(inside))
    def _():
        product = jnp.zeros((rows, TILE), jnp.float32)
        for k, ref in enumerate((first_ref, second_ref)):
            panel_top, panel_rest = halves(ref[...])
            top = top_ref[:, k * TILE : (k + 1) * TILE]
            rest = rest_ref[:, k * TILE : (k + 1) * TILE]
            product += dot_nt(top, panel_top) + (dot_nt(top, panel_rest) + dot_nt(rest, panel_top))
        out_ref[...] = jnp.where(kept, rows_ref[...] - product, 0.0)


def finish(rows_mat, first, second, weights, first_row):
    rows, order = rows_mat.shape
    low, high = order - 3 * TILE, order - TILE
    return pl.pallas_call(
        functools.partial(finish_kernel, low, high),
        out_shape=jax.ShapeDtypeStruct(rows_mat.shape, jnp.float32),
        grid_spec=pltpu.PrefetchScalarGridSpec(
            num_scalar_prefetch=1,
            grid=(order // TILE,),
            in_specs=[
                pl.BlockSpec((rows, TILE), lambda n, _: (0, n)),
                pl.BlockSpec((TILE, TILE), lambda n, _: (n, 0)),
                pl.BlockSpec((TILE, TILE), lambda n, _: (n, 0)),
                pl.BlockSpec((rows, 2 * TILE), lambda n, _: (0, 0)),
            ],
            out_specs=pl.BlockSpec((rows, TILE), lambda n, _: (0, n)),
            scratch_shapes=[pltpu.VMEM((rows, 2 * TILE), jnp.bfloat16)] * 2,
        ),
        compiler_params=pltpu.CompilerParams(vmem_limit_bytes=24 * MIB),
        cost_estimate=pl.CostEstimate(
            flops=2 * rows * order * TILE * 6, bytes_accessed=rows * order * 16, transcendentals=0
        ),
    )(first_row, rows_mat, first, second, weights)


def product(left, right, precision=HIGHEST):
    return jnp.dot(left, right, precision=precision, preferred_element_type=jnp.float32)


def product_nt(left, right, precision=HIGHEST):
    return lax.dot_general(left, right, NT, precision=precision, preferred_element_type=jnp.float32)


def swap(value, mask):
    pairs = [(source, source ^ mask) for source in range(lax.axis_size("cube"))]
    return lax.ppermute(value, "cube", pairs)


def group_gather(value, group):
    size = lax.axis_size("cube")
    groups = [[g * group + i for i in range(group)] for g in range(size // group)]
    return lax.all_gather(value, "cube", axis=0, tiled=True, axis_index_groups=groups)


def one_hot(positions, count):
    return (positions[None, :] == jnp.arange(count, dtype=jnp.int32)[:, None]).astype(jnp.float32)


def column_targets(front_map):
    order = front_map.shape[0]
    ids = jnp.arange(order, dtype=jnp.int32)
    gone = (ids >= order - 2 * TILE) & (ids < order - TILE)
    return jnp.where(gone, -1, front_map)


class Plan:
    def __init__(self, maps, group, rows):
        me = lax.axis_index("cube")
        front = me // group
        block = me % group
        side = front % 2
        self.own_map = column_targets(lax.dynamic_index_in_dim(maps, front, 0, keepdims=False))
        self.other_map = column_targets(lax.dynamic_index_in_dim(maps, front ^ 1, 0, keepdims=False))
        own = lax.dynamic_slice_in_dim(self.own_map, block * rows, rows, 0)
        other = lax.dynamic_slice_in_dim(self.other_map, block * rows, rows, 0)
        here = (block + group * side) * rows
        there = (block + group * (1 - side)) * rows
        self.keep = one_hot(own - here, rows)
        self.give = one_hot(own - there, rows)
        leaves = (own >= there) & (own < there + rows)
        rank = jnp.where(leaves, jnp.cumsum(leaves.astype(jnp.int32)) - 1, -1)
        self.send = one_hot(rank, rows)
        comes = (other >= here) & (other < here + rows)
        rank = jnp.where(comes, jnp.cumsum(comes.astype(jnp.int32)) - 1, -1)
        self.place = lax.dot_general(one_hot(other - here, rows), one_hot(rank, rows), NT).astype(jnp.bfloat16)


def local(gfront, cfront, rfront, gmap, cmap):
    devices = lax.axis_size("cube")
    me = lax.axis_index("cube")
    quarter = devices // 4
    half = devices // 2
    rows = gfront.shape[0]
    order_g, order_c, order_r = gfront.shape[1], cfront.shape[1], rfront.shape[1]
    g_low, c_low = order_g - 2 * TILE, order_c - 2 * TILE
    r_low = order_r - 3 * TILE
    plan_g = Plan(gmap, quarter, rows)
    plan_c = Plan(cmap, half, rows)

    own_g = gfront[:, g_low : g_low + TILE]
    own_c = cfront[:, c_low : c_low + TILE]
    panel_g = group_gather(own_g, quarter)
    panel_c = group_gather(own_c, half)
    second = lax.all_gather(rfront[:, r_low + TILE : r_low + 2 * TILE], "cube", axis=0, tiled=True)
    diag = jnp.stack([panel_g[g_low : g_low + TILE], panel_c[c_low : c_low + TILE]])
    inverse = inverse_factors(diag)

    def factors(own, inv, order):
        factor = product_nt(own, inv)
        weights = product(factor, inv)
        row_ids = me * rows % order + jnp.arange(rows, dtype=jnp.int32)
        low = order - 2 * TILE
        return factor, weights, row_ids

    gfactor, weights_g, _ = factors(own_g, inverse[0], order_g)
    cfactor, weights_c, _ = factors(own_c, inverse[1], order_c)

    g_edge = gfront[:, g_low - TILE : g_low] - product_nt(weights_g, panel_g[g_low - TILE : g_low])
    edge_map = plan_g.own_map[g_low - TILE : g_low]
    g_edge = product_nt(g_edge, one_hot(edge_map - (c_low - TILE), TILE))
    c_edge = cfront[:, c_low - TILE : c_low] - product_nt(weights_c, panel_c[c_low - TILE : c_low])
    c_edge = c_edge + product(plan_g.keep, g_edge) + swap(product(plan_g.give, g_edge), quarter)
    edge_map = plan_c.own_map[c_low - TILE : c_low]
    c_edge = product_nt(c_edge, one_hot(edge_map - r_low, TILE))
    r_edge = rfront[:, r_low : r_low + TILE]
    r_edge = r_edge + product(plan_c.keep, c_edge) + swap(product(plan_c.give, c_edge), half)
    first = lax.all_gather(r_edge, "cube", axis=0, tiled=True)

    g_done = gfront - product_nt(weights_g, panel_g, HIGH)
    g_recv = swap(product(plan_g.send, g_done, HIGH), quarter)
    g_keep = product(plan_g.keep, g_done, HIGH)
    c_base = cfront - product_nt(weights_c, panel_c, HIGH)
    c_done = assemble(
        c_base, g_keep, g_recv, plan_g.place, plan_g.own_map[None], plan_g.other_map[None]
    )
    c_recv = swap(product(plan_c.send, c_done, HIGH), half)
    c_keep = product(plan_c.keep, c_done, HIGH)
    r_rows = assemble(
        rfront, c_keep, c_recv, plan_c.place, plan_c.own_map[None], plan_c.other_map[None]
    )

    r_high = r_low + TILE
    inv_11 = inverse_factors(first[r_low:r_high][None])[0]
    low_21 = product_nt(first[r_high : r_high + TILE], inv_11)
    inv_22 = inverse_factors((second[r_high : r_high + TILE] - product_nt(low_21, low_21))[None])[0]
    inv_21 = -product(inv_22, product(low_21, inv_11))
    own_first, own_second = r_edge, rfront[:, r_high : r_high + TILE]
    factor_1 = product_nt(own_first, inv_11)
    factor_2 = product_nt(own_first, inv_21) + product_nt(own_second, inv_22)
    weights_1 = product(factor_1, inv_11) + product(factor_2, inv_21)
    weights_2 = product(factor_2, inv_22)
    row_ids = me * rows + jnp.arange(rows, dtype=jnp.int32)
    above = (row_ids >= r_low) & (row_ids < r_high)
    factor_2 = jnp.where(above[:, None], 0.0, factor_2)
    rfactor = jnp.concatenate([factor_1, factor_2], 1)
    first_row = (me * rows).astype(jnp.int32).reshape(1)
    rschur = finish(r_rows, first, second, jnp.concatenate([weights_1, weights_2], 1), first_row)
    return (gfactor, cfactor, rfactor, rschur)


def solution(mesh):
    placed = (P("cube", None), P("cube", None), P("cube", None), P(), P())
    return jax.shard_map(
        local,
        mesh=mesh,
        in_specs=placed,
        out_specs=(P("cube", None), P("cube", None), P("cube", None), P("cube", None)),
        check_vma=False,
    )
```

time: 1290 us -> 539 us (0.42)
  waiting for transfers between devices: 760 us -> 351 us
  other arithmetic: 309 us -> 4.06 us
  local copies, waits for them, and re-layouts: 124 us -> 29.7 us
  Pallas kernels: 0 us -> 88.7 us
  matrix products: 68.8 us -> 36.2 us
    all_gather x4, waiting for transfers between devices: 335 us -> 64.6 us  [the longest x2 64.5 us: group_gather(): lax.all_gather(value, 'cube', axis=0, tiled=True, axis_index_groups=groups)]
    another operation x36 -> x11, other arithmetic: 217 us -> 1.59 us  [the longest x27 138 us: eliminate(): lower_tri = jnp.linalg.cholesky(whole_panel[col_low:col_high])]
    ppermute x2 -> x4, waiting for transfers between devices: 425 us -> 287 us  [swap(): return lax.ppermute(value, 'cube', pairs)]
    pallas_call x0 -> x6, Pallas kernels: none -> 88.7 us  [the longest x2 40.4 us: assemble(): pl.pallas_call(assemble_kernel, grid=(order // TILE,), out_shape=jax.Shap...]
    scatter-add x4 -> x0, other arithmetic: 72.1 us -> none  [the longest x2 40.9 us: extend_add(): jnp.zeros((row_count, 2 * order), jnp.float32).at[:, own_map].add(masked)]
    unnamed x19 -> x23, local copies, waits for them, and re-layouts: 65 us -> 21 us
    dot_general x4 -> x30, matrix products: 58.3 us -> 36.2 us  [the longest x15 18.7 us: product(): jnp.dot(left, right, precision=precision, preferred_element_type=jnp.floa...]
    dynamic_slice x2 -> x0, local copies, waits for them, and re-layouts: 18.9 us -> none  [extend_add(): lax.dynamic_slice_in_dim(own_pair, side * row_count, row_count, 0)]
  transfers between devices with their start and end apart: 6 -> 8, of which waited for: 6 -> 6; matrix products, arithmetic and copies ran while one was open for 3% -> 7% of each run, Pallas kernels for 0% -> 9%
where the time goes in v1:
time: 539 us; the launch traced here: 528 us
  waiting for transfers between devices  351 us (65%)
  Pallas kernels  88.7 us (16%)
  matrix products  36.2 us (7%)
  local copies, waits for them, and re-layouts  29.7 us (6%)
  between operations  14.5 us (3%)
    ppermute x4, waiting for transfers between devices, swap(): return lax.ppermute(value, 'cube', pairs)  287 us
    all_gather x2, waiting for transfers between devices, group_gather(): lax.all_gather(value, 'cube', axis=0, tiled=True, axis_index_groups=groups)  64.5 us
    pallas_call x2, Pallas kernels, assemble(): pl.pallas_call(assemble_kernel, grid=(order // TILE,), out_shape=jax.Shap...  40.4 us
    pallas_call x3, Pallas kernels, inverse_factors(): pl.pallas_call(functools.partial(inverse_kernel, count), out_shape=jax.Sh...  29.5 us
    unnamed x23, local copies, waits for them, and re-layouts  21 us
    pallas_call x1, Pallas kernels, finish(): pl.pallas_call(functools.partial(finish_kernel, low, high), out_shape=jax...  18.7 us
    dot_general x15, matrix products, product(): jnp.dot(left, right, precision=precision, preferred_element_type=jnp.floa...  18.7 us
    dot_general x13, matrix products, product_nt(): lax.dot_general(left, right, NT, precision=precision, preferred_element_t...  17 us
  transfers between devices with their start and end apart: 8, of which 6 were waited for; matrix products, arithmetic and copies ran while one was open for 7% of the time, Pallas kernels for 9%

profile of v1, /device:TPU:0, one launch (start us, length us, event | category | flops | bytes accessed | tf_op | source)
XLA Modules:
  0.0 528.3 jit_solution(3426371360964876441)
XLA Ops:
  12.7 28.4 %all-gather.5.cloned.1.call-done = f32[2048,256]{1,0:T(8,128)} async-done(((f32[256,256]{1,0:T(8,128)}), f32[2048,256]{1,0:T(8,128)}) %all-gather.5.cloned.1.call-update) | async-done | bytes 2097168 | tf_op jit(solution)/shard_map/all_gather | solution.py:213
  42.1 36.2 %all-gather.7.cloned.1.call-done = f32[4096,256]{1,0:T(8,128)} async-done(((f32[256,256]{1,0:T(8,128)}), f32[4096,256]{1,0:T(8,128)}) %all-gather.7.cloned.1.call-update) | async-done | bytes 4194320 | tf_op jit(solution)/shard_map/all_gather | solution.py:213
  79.3 10.6 %shard_map.84 = f32[2,256,256]{2,1,0:T(8,128)S(1)} custom-call(f32[2,256,256]{2,1,0:T(8,128)S(1)} %pad_maximum_fusion.blocks_ref), custom_call_target="tpu_custom_call" | custom-call | flops 30000001024 | bytes 1000000 | tf_op jit(solution)/shard_map/pallas_call | solution.py:83
  97.4 5.5 %collective-permute-done = f32[256,256]{1,0:T(8,128)S(1)} collective-permute-done((f32[256,256]{1,0:T(8,128)S(1)}, f32[256,256]{1,0:T(8,128)S(1)}, u32[]{:S(2)}, u32[]{:S(2)}) %collective-permute-start) | collective-permute-done | bytes 262176 | tf_op jit(solution)/shard_map/ppermute | solution.py:207
  103.8 2.5 collective-permute-start.1
  106.3 11.7 %collective-permute-done.1 = f32[256,256]{1,0:T(8,128)S(1)} collective-permute-done((f32[256,256]{1,0:T(8,128)S(1)}, f32[256,256]{1,0:T(8,128)S(1)}, u32[]{:S(2)}, u32[]{:S(2)}) %collective-permute-start.1) | collective-permute-done | bytes 262176 | tf_op jit(solution)/shard_map/ppermute | solution.py:207
  122.9 2.7 convolution_subtract_fusion.1
  126.9 2.1 fusion.24
  130.2 2.7 fusion.18.keep_ref
  133.0 4.1 convolution_subtract_fusion.base_ref
  137.1 78.1 %collective-permute-done.2.recv_ref = f32[256,2048]{1,0:T(8,128)S(1)} collective-permute-done((f32[256,2048]{1,0:T(8,128)}, f32[256,2048]{1,0:T(8,128)S(1)}, u32[]{:S(2)}, u32[]{:S(2)}) %collective-permute-start.2) | collective-permute-done | bytes 2097184 | tf_op jit(solution)/shard_map/ppermute | solution.py:207
  215.2 12.1 %shard_map.87 = f32[256,4096]{1,0:T(8,128)S(1)} custom-call(f32[256,4096]{1,0:T(8,128)S(1)} %convolution_subtract_fusion.base_ref, f32[256,2048]{1,0:T(8,128)S(1)} %fusion.18.keep_ref, f32[256,2048]{1,0:T(8,128)S(1)} %collective-permute-done.2.recv_ref, bf16[256,256]{1,0:T(8,128)(2,1)S(1)} %convolution_convert_fusion.1.place_ref, ...), custom_call_target="tpu_custom_call" | custom-call | flops 3221225472 | bytes 12582912 | tf_op jit(solution)/shard_map/pallas_call | solution.py:125
  227.3 3.4 fusion.25
  233.7 3.6 fusion.19.keep_ref
  237.3 191.5 %collective-permute-done.3.recv_ref = f32[256,4096]{1,0:T(8,128)} collective-permute-done((f32[256,4096]{1,0:T(8,128)}, f32[256,4096]{1,0:T(8,128)}, u32[]{:S(2)}, u32[]{:S(2)}) %collective-permute-start.3) | collective-permute-done | bytes 4194336 | tf_op jit(solution)/shard_map/ppermute | solution.py:207
  428.9 3.4 copy-done.3
  432.3 28.3 %shard_map.88.rows_ref = f32[256,8192]{1,0:T(8,128)S(1)} custom-call(f32[256,8192]{1,0:T(8,128)S(1)} %copy-done.3, f32[256,4096]{1,0:T(8,128)S(1)} %fusion.19.keep_ref, f32[256,4096]{1,0:T(8,128)} %collective-permute-done.3.recv_ref, bf16[256,256]{1,0:T(8,128)(2,1)S(1)} %convolution_convert_fusion.place_ref, s32[1,4096]{1,0:T(1,128)S(1)} %get-tuple-element.28.keep_map_ref, ...), custom_call_target="tpu_custom_call" | custom-call | flops 6442450944 | bytes 25165824 | tf_op jit(solution)/shard_map/pallas_call | solution.py:125
  460.6 3.4 copy-done.1
  465.0 9.4 %shard_map.85 = f32[1,256,256]{2,1,0:T(8,128)S(1)} custom-call(f32[1,256,256]{2,1,0:T(8,128)S(1)} %slice_bitcast_fusion.blocks_ref), custom_call_target="tpu_custom_call" | custom-call | flops 30000001024 | bytes 1000000 | tf_op jit(solution)/shard_map/pallas_call | solution.py:83
  478.6 9.6 %shard_map.86 = f32[1,256,256]{2,1,0:T(8,128)S(1)} custom-call(f32[1,256,256]{2,1,0:T(8,128)S(1)} %fusion.blocks_ref), custom_call_target="tpu_custom_call" | custom-call | flops 30000001024 | bytes 1000000 | tf_op jit(solution)/shard_map/pallas_call | solution.py:83
  492.6 3.4 copy-done.2
  496.0 3.4 copy-done.4
  499.4 3.4 copy-done.5
  502.8 18.7 %shard_map.89 = f32[256,8192]{1,0:T(8,128)} custom-call(s32[1]{0:T(128)} %bitcast.13.base_ref, f32[256,8192]{1,0:T(8,128)S(1)} %copy-done.2, f32[8192,256]{1,0:T(8,128)S(1)} %copy-done.4, f32[8192,256]{1,0:T(8,128)S(1)} %copy-done.5, f32[256,512]{1,0:T(8,128)S(1)} %pad_maximum_fusion.2.weights_ref), custom_call_target="tpu_custom_call" | custom-call | flops 6442450944 | bytes 33554432 | tf_op jit(solution)/shard_map/pallas_call | solution.py:175
  (97 shorter events, 35.7 us)
Async XLA Ops:
  7.2 33.9 %all-gather.5.cloned.1.call-start = ((), (), s32[]{:S(2)}) async-start(), calls=%async_computation | async-start | bytes 2359296 | tf_op jit(solution)/shard_map/all_gather | solution.py:213
  8.9 69.3 %all-gather.7.cloned.1.call-start = ((), (), s32[]{:S(2)}) async-start(), calls=%async_computation.1 | async-start | bytes 4456448 | tf_op jit(solution)/shard_map/all_gather | solution.py:213
  10.7 453.4 %all-gather.9.cloned.1.call-start = ((), (), s32[]{:S(2)}) async-start(), calls=%async_computation.2 | async-start | bytes 8650752 | tf_op jit(solution)/shard_map/all_gather | solution.py:288
  79.3 12.0 %copy-start.9 = (f32[256,2048]{1,0:T(8,128)S(1)}, f32[256,2048]{1,0:T(8,128)}, u32[]{:S(2)}) copy-start(f32[256,2048]{1,0:T(8,128)} %param.5) | copy-start | bytes 6291460
  94.3 8.5 %collective-permute-start = (f32[256,256]{1,0:T(8,128)S(1)}, f32[256,256]{1,0:T(8,128)S(1)}, u32[]{:S(2)}, u32[]{:S(2)}) collective-permute-start(f32[256,256]{1,0:T(8,128)S(1)} %fusion.21), channel_id=1, source_target_pairs={{0,8},{1,9},{2,10},{3,11},{4,12},{5,13},{6,14},{7,15},{8,0},{9,1},... | collective-permute-start | bytes 786440 | tf_op jit(solution)/shard_map/ppermute | solution.py:207
  103.8 14.2 %collective-permute-start.1 = (f32[256,256]{1,0:T(8,128)S(1)}, f32[256,256]{1,0:T(8,128)S(1)}, u32[]{:S(2)}, u32[]{:S(2)}) collective-permute-start(f32[256,256]{1,0:T(8,128)S(1)} %fusion.23), channel_id=1, source_target_pairs={{0,16},{1,17},{2,18},{3,19},{4,20},{5,21},{6,22},{7,23},{8,24},{9,... | collective-permute-start | bytes 786440 | tf_op jit(solution)/shard_map/ppermute | solution.py:207
  120.0 357.2 %all-gather.11.cloned.1.call-start = ((), (), s32[]{:S(2)}) async-start(), calls=%async_computation.3 | async-start | bytes 8650752 | tf_op jit(solution)/shard_map/all_gather | solution.py:265
  125.6 1.3 copy-start.6
  129.0 86.1 %collective-permute-start.2 = (f32[256,2048]{1,0:T(8,128)}, f32[256,2048]{1,0:T(8,128)S(1)}, u32[]{:S(2)}, u32[]{:S(2)}) collective-permute-start(f32[256,2048]{1,0:T(8,128)} %fusion.24), channel_id=1, source_target_pairs={{0,8},{1,9},{2,10},{3,11},{4,12},{5,13},{6,14},{7,15},{8,0},{9,1},... | collective-permute-start | bytes 6291464 | tf_op jit(solution)/shard_map/ppermute | solution.py:207
  129.5 3.4 copy-start.7
  227.3 3.4 copy-start
  230.7 198.2 %collective-permute-start.3 = (f32[256,4096]{1,0:T(8,128)}, f32[256,4096]{1,0:T(8,128)}, u32[]{:S(2)}, u32[]{:S(2)}) collective-permute-start(f32[256,4096]{1,0:T(8,128)} %fusion.25), channel_id=1, source_target_pairs={{0,16},{1,17},{2,18},{3,19},{4,20},{5,21},{6,22},{7,23},{8,24},{9,... | collective-permute-start | bytes 12582920 | tf_op jit(solution)/shard_map/ppermute | solution.py:207
  428.8 3.4 copy-start.3
  460.6 3.4 copy-start.1
  465.0 9.4 %copy-start.8 = (f32[256,256]{1,0:T(8,128)S(1)}, f32[256,256]{1,0:T(8,128)}, u32[]{:S(2)}) copy-start(f32[256,256]{1,0:T(8,128)} %fusion.1) | copy-start | bytes 786436
  492.6 3.4 copy-start.2
  496.0 3.4 copy-start.4
  499.4 3.4 copy-start.5
Sparse Core Ops, SparseCore 0:
  10.5 30.5 all-gather.4
  43.3 34.9 all-gather.6
  120.1 96.5 all-gather.8
  219.4 242.4 all-gather.10
